TPU v7x, 512 devices: a whole 4x8x8 slice. The times are simulated.
512 devices in a mesh: dp: 16 (over y_lo, x, core), expert: 32 (over y_hi, z).
Axes of the slice: x: 4, y: 8 (y_hi: 4, y_lo: 2; y = y_hi * 2 + y_lo), z: 8, core: 2. Of those that a mesh axis runs over, the one named last changes fastest.
Arguments:
- events: bfloat16 [1024, 1024], P(('dp', 'expert')), may hold values from -6 to 6
- labels: int32 [1024, 4], P(('dp', 'expert')), may hold values 0 or 1
- w_in: bfloat16 [32, 1024, 4096], P('expert', None, 'dp'), may hold values from -0.1875 to 0.1875
- w_out: bfloat16 [32, 4096, 1024], P('expert', 'dp'), may hold values from -0.09375 to 0.09375
- gate_weight: bfloat16 [4, 1024, 32], replicated, may hold values from -4 to 4
- tower_in: bfloat16 [4, 1024, 256], replicated, may hold values from -0.1875 to 0.1875
- tower_bias: float32 [4, 256], replicated, may hold values from -3 to 3
- tower_out: float32 [4, 256], replicated, may hold values from -0.75 to 0.75
- tower_out_bias: float32 [4], replicated, may hold values from -3 to 3
Outputs:
- grad_in: bfloat16 [32, 1024, 4096], P('expert', None, 'dp')
- grad_out: bfloat16 [32, 4096, 1024], P('expert', 'dp')
- grad_gate: float32 [4, 1024, 32], P(None, None, 'expert')
All inputs are finite; a program needn't handle non-finite values. No bound on the sum of `labels` on one device may be relied on, other than what follows from the above.
Results may differ from a plain program's by a relative error of at most 0.035.
Values may be sent and summed in bfloat16 or wider, within the bound.
A program may use at most 64 MiB of HBM per device.

v0:
```python
import jax
import jax.numpy as jnp
from jax import lax
from jax.sharding import PartitionSpec as P


def gelu_tanh(value):
    return jax.nn.gelu(value, approximate=True)


def tower_apply(mixed, tower_in, tower_bias, tower_out, tower_out_bias):
    tower_pre = (
        jnp.einsum(
            "trd,tdk->trk", mixed, tower_in.astype(jnp.float32), precision=lax.Precision.HIGHEST
        )
        + tower_bias[:, None, :]
    )
    return jnp.sum(gelu_tanh(tower_pre) * tower_out[:, None, :], -1) + tower_out_bias[:, None]


def per_device(
    events, labels, w_in, w_out, gate_weight, tower_in, tower_bias, tower_out, tower_out_bias
):
    experts_here = lax.axis_size("expert")
    own_rows = events.shape[0]
    every = lax.all_gather(events, ("dp", "expert"), axis=0, tiled=True)
    span = own_rows * experts_here
    dp_index = lax.axis_index("dp")
    expert_index = lax.axis_index("expert")
    pre = jnp.dot(every, w_in[0], preferred_element_type=jnp.float32)
    hidden = gelu_tanh(pre).astype(jnp.bfloat16)
    expert_out = lax.psum_scatter(
        jnp.dot(hidden, w_out[0], preferred_element_type=jnp.float32).astype(jnp.bfloat16),
        "dp",
        scatter_dimension=0,
        tiled=True,
    )
    targets = labels.T.astype(jnp.float32)

    def tower_of(value):
        return tower_apply(value, tower_in, tower_bias, tower_out, tower_out_bias)

    block_rows = lax.dynamic_slice_in_dim(every, dp_index * span, span, 0)
    gate_logits = jnp.einsum(
        "rd,tde->tre", block_rows, gate_weight, preferred_element_type=jnp.float32
    )
    probs = jax.nn.softmax(gate_logits, axis=-1)
    own_prob = lax.dynamic_slice_in_dim(probs, expert_index, 1, 2)[:, :, 0]
    outs_wide = expert_out.astype(jnp.float32)
    terms = own_prob[:, :, None] * outs_wide[None]
    mixed = lax.psum_scatter(terms.astype(jnp.bfloat16), "expert", scatter_dimension=1, tiled=True)
    logit, tower_back = jax.vjp(tower_of, mixed.astype(jnp.float32))
    dmixed = tower_back(jax.nn.sigmoid(logit) - targets)[0].astype(jnp.bfloat16)
    block_grads = lax.all_gather(dmixed, "expert", axis=1, tiled=True)
    dprob = jnp.einsum("trd,rd->tr", block_grads, expert_out, preferred_element_type=jnp.float32)
    weighted = lax.psum(own_prob * dprob, "expert")
    dgate = own_prob * (dprob - weighted)
    grads_wide = block_grads.astype(jnp.float32)
    dexpert = jnp.einsum(
        "tr,trd->rd", own_prob, grads_wide, precision=lax.Precision.HIGHEST
    ).astype(jnp.bfloat16)
    gate_part = jnp.einsum(
        "rd,tr->td", block_rows.astype(jnp.float32), dgate, precision=lax.Precision.HIGHEST
    )
    grad_gate = lax.psum(gate_part, "dp")[:, :, None]
    all_grads = lax.all_gather(dexpert, "dp", axis=0, tiled=True)
    dhidden = lax.dot_general(
        all_grads, w_out[0], (((1,), (1,)), ((), ())), preferred_element_type=jnp.float32
    )
    gelu_back = jax.vjp(gelu_tanh, pre)[1]
    dpre = gelu_back(dhidden)[0].astype(jnp.bfloat16)
    grad_second = lax.dot_general(
        hidden, all_grads, (((0,), (0,)), ((), ())), preferred_element_type=jnp.float32
    ).astype(jnp.bfloat16)
    grad_first = lax.dot_general(
        every, dpre, (((0,), (0,)), ((), ())), preferred_element_type=jnp.float32
    ).astype(jnp.bfloat16)
    return (grad_first[None], grad_second[None], grad_gate)


def solution(mesh):
    placed = (
        P(("dp", "expert"), None),
        P(("dp", "expert"), None),
        P("expert", None, "dp"),
        P("expert", "dp", None),
        P(),
        P(),
        P(),
        P(),
        P(),
    )
    return jax.shard_map(
        per_device,
        mesh=mesh,
        in_specs=placed,
        out_specs=(P("expert", None, "dp"), P("expert", "dp", None), P(None, None, "expert")),
        check_vma=False,
    )
```

profile of v0, /device:TPU:1, one launch (start us, length us, event | category | flops | bytes accessed | tf_op | source)
XLA Modules:
  0.0 1696.0 jit_solution(13579556449871129336)
XLA Ops:
  7.2 0.0 copy-start
  7.2 0.0 all-gather.6.cloned.1.call-start
  7.2 0.7 all-gather.6.cloned.1.call-update
  7.9 0.0 copy-start.7
  7.9 0.0 reduce-scatter.2.cloned.1.call-start
  8.0 1060.3 %all-gather.6.cloned.1.call-done = bf16[512,2,1024]{2,1,0:T(2,128)(2,1)} async-done(((bf16[1,2,1024]{2,1,0:T(2,128)(2,1)}), bf16[512,2,1024]{2,1,0:T(2,128)(2,1)}) %all-gather.6.cloned.1.call-update) | async-done | bytes 2097168 | tf_op jit(solution)/shard_map/all_gather | solution.py:26
  1068.2 4.1 reshape.13
  1072.3 0.0 copy-done.7
  1072.3 0.0 copy-start.8
  1072.3 2.4 fusion.17
  1074.7 0.0 copy-start.9
  1074.7 1.0 copy-done.9
  1075.7 0.0 copy-done.8
  1075.7 0.0 copy-start.1
  1075.7 2.1 convolution_convert_fusion
  1077.8 0.0 copy-start.5
  1077.8 0.0 copy-start.3
  1077.8 0.0 copy-start.4
  1077.8 0.0 reduce-scatter.2.cloned.1.call-update
  1077.8 0.0 all-reduce.3.cloned.1.call-start
  1077.9 0.0 copy-done.1
  1077.9 1.1 fusion.28
  1079.0 0.0 copy-start.6
  1079.0 0.2 fusion.78
  1079.2 0.1 copy.23
  1079.3 63.1 %reduce-scatter.2.cloned.1.call-done = bf16[64,1024]{1,0:T(8,128)(2,1)} async-done(((bf16[1024,1024]{1,0:T(8,128)(2,1)}), bf16[64,1024]{1,0:T(8,128)(2,1)}) %reduce-scatter.2.cloned.1.call-update) | async-done | bytes 131088 | tf_op jit(solution)/shard_map/reduce_scatter | solution.py:32
  1142.4 0.9 convert_element_type.42
  1143.3 1.0 multiply_convert_fusion
  1144.3 0.0 all-reduce.3.cloned.1.call-update
  1144.4 0.0 all-gather.4.cloned.1.call-start
  1144.4 0.0 copy-done.5
  1144.4 0.1 copy.25
  1144.5 1.3 dynamic-slice
  1146.4 0.1 copy.29
  1146.5 294.9 %all-reduce.3.cloned.1.call-done = bf16[4,64,1024]{2,0,1:T(4,128)(2,1)} async-done(((bf16[4,64,1024]{2,0,1:T(4,128)(2,1)}), bf16[4,64,1024]{2,0,1:T(4,128)(2,1)}) %all-reduce.3.cloned.1.call-update) | async-done | bytes 524304
  1441.5 0.7 constant_dynamic-slice_fusion
  1442.2 0.0 copy-done
  1442.2 0.0 copy-done.3
  1442.2 0.0 copy-done.4
  1442.2 0.5 multiply_reduce_fusion
  1442.7 0.0 copy-done.6
  1442.7 0.1 divide_subtract_fusion
  1442.8 0.0 copy-start.2
  1442.8 1.8 convolution_convert_fusion.3
  1444.6 70.3 %all_gather.10 = bf16[4,64,1024]{2,0,1:T(4,128)(2,1)S(1)} all-gather(bf16[4,2,1024]{2,0,1:T(4,128)(2,1)S(1)} %copy.26), channel_id=1, replica_groups=mesh['dp'=16,'expert'=32] {'expert'}, dimensions={1}, use_global_device_ids=true | all-gather | bytes 540672 | tf_op jit(solution)/shard_map/all_gather | solution.py:54
  1514.8 1.0 fusion.79
  1515.8 0.7 copy.40
  1516.5 0.0 all-gather.4.cloned.1.call-update
  1516.5 0.0 copy-done.2
  1516.5 0.6 fusion.25
  1517.2 0.1 copy.32
  1517.2 63.3 %psum.14 = f32[4,64]{1,0:T(4,128)S(1)} all-reduce(f32[4,64]{1,0:T(4,128)S(1)} %bitcast_multiply_fusion), channel_id=1, replica_groups=mesh['dp'=16,'expert'=32] {'expert'}, use_global_device_ids=true, to_apply=%region_5.0 | all-reduce | flops 256 | bytes 2048 | tf_op jit(solution)/shard_map/psum | solution.py:56
  1580.5 1.1 convolution_bitcast_fusion
  1581.6 97.6 %psum.15 = f32[4,1024,1]{1,0,2:T(4,128)S(1)} all-reduce(f32[4,1024,1]{1,0,2:T(4,128)S(1)} %convolution_bitcast_fusion), channel_id=1, replica_groups=mesh['dp'=16,'expert'=32] {'dp'}, use_global_device_ids=true, to_apply=%region_6.0 | all-reduce | flops 4096 | bytes 32768 | tf_op jit(solution)/shard_map/psum | solution.py:65
  1679.1 0.6 copy.28
  1679.8 0.0 all-gather.4.cloned.1.call-done
  1679.8 5.2 fusion
  1685.0 1.0 copy.27
  1686.0 3.5 fusion.1
  (3 shorter events, 0.0 us)
Async XLA Ops:
  7.2 1435.0 %copy-start = (bf16[4,1024,256]{2,1,0:T(8,128)(2,1)S(1)}, bf16[4,1024,256]{2,1,0:T(8,128)(2,1)}, u32[]{:S(2)}) copy-start(bf16[4,1024,256]{2,1,0:T(8,128)(2,1)} %param.14) | copy-start | bytes 6291460
  7.2 1061.0 %all-gather.6.cloned.1.call-start = ((), (), s32[]{:S(2)}) async-start(), calls=%async_computation.3 | async-start | bytes 2101248 | tf_op jit(solution)/shard_map/all_gather | solution.py:26
  7.9 1064.4 %copy-start.7 = (bf16[1,1024,256]{2,1,0:T(8,128)(2,1)S(1)}, bf16[1,1024,256]{2,1,0:T(8,128)(2,1)}, u32[]{:S(2)}) copy-start(bf16[1,1024,256]{2,1,0:T(8,128)(2,1)} %param.11) | copy-start | bytes 1572868
  7.9 1134.4 %reduce-scatter.2.cloned.1.call-start = ((), (), s32[]{:S(2)}) async-start(), calls=%async_computation.1 | async-start | bytes 2228224 | tf_op jit(solution)/shard_map/reduce_scatter | solution.py:32
  1072.3 3.3 copy-start.8
  1074.7 1.0 copy-start.9
  1075.7 2.2 copy-start.1
  1077.8 66.6 %copy-start.5 = (s32[2,4]{1,0:T(2,128)S(1)}, s32[2,4]{1,0:T(2,128)}, u32[]{:S(2)}) copy-start(s32[2,4]{1,0:T(2,128)} %param.10) | copy-start | bytes 100
  1077.8 364.4 %copy-start.3 = (f32[4,256]{1,0:T(4,128)S(1)}, f32[4,256]{1,0:T(4,128)}, u32[]{:S(2)}) copy-start(f32[4,256]{1,0:T(4,128)} %param.16) | copy-start | bytes 12292
  1077.8 364.4 %copy-start.4 = (f32[4,256]{1,0:T(4,128)S(1)}, f32[4,256]{1,0:T(4,128)}, u32[]{:S(2)}) copy-start(f32[4,256]{1,0:T(4,128)} %param.15) | copy-start | bytes 12292
  1077.8 363.6 %all-reduce.3.cloned.1.call-start = ((), (), s32[]{:S(2)}) async-start(), calls=%async_computation.4 | async-start | bytes 1048576
  1079.0 363.7 %copy-start.6 = (f32[4]{0:T(128)S(1)}, f32[4]{0:T(128)}, u32[]{:S(2)}) copy-start(f32[4]{0:T(128)} %param.17) | copy-start | bytes 52
  1144.4 535.4 %all-gather.4.cloned.1.call-start = ((), (), s32[]{:S(2)}) async-start(), calls=%async_computation.2 | async-start | bytes 2228224 | tf_op jit(solution)/shard_map/all_gather | solution.py:66
  1442.8 73.7 %copy-start.2 = (bf16[64,1024]{1,0:T(8,128)(2,1)S(1)}, bf16[64,1024]{1,0:T(8,128)(2,1)}, u32[]{:S(2)}) copy-start(bf16[64,1024]{1,0:T(8,128)(2,1)} %reduce-scatter.2.cloned.1.call-done) | copy-start | bytes 393220
Sparse Core Ops, SparseCore 0:
  10.2 1058.0 all-gather.5
  1077.9 64.3 reduce-scatter.1
  1145.9 295.5 all-reduce.2
  1516.6 67.3 all-gather.3
where the time goes:
time: 1700 us
  waiting for transfers between devices  1420 us (84%)
  blocking collectives  231 us (14%)
  matrix products  19.3 us (1%)
    all_gather x1, waiting for transfers between devices, per_device(): every = lax.all_gather(events, ('dp', 'expert'), axis=0, tiled=True)  1060 us
    unnamed x5, waiting for transfers between devices  296 us
    psum x1, blocking collectives, per_device(): grad_gate = lax.psum(gate_part, 'dp')[:, :, None]  97.6 us
    all_gather x1, blocking collectives, per_device(): block_grads = lax.all_gather(dmixed, 'expert', axis=1, tiled=True)  70.3 us
    psum x1, blocking collectives, per_device(): weighted = lax.psum(own_prob * dprob, 'expert')  63.3 us
    reduce_scatter x1, waiting for transfers between devices, per_device(): lax.psum_scatter(jnp.dot(hidden, w_out[0], preferred_element_type=jnp.flo...  63.1 us
  transfers between devices with their start and end apart: 4, of which 3 were waited for; matrix products, arithmetic and copies ran while one was open for 0% of the time, Pallas kernels for 0%

commit v1 on v0

v1 whole, which is shorter than its diff:
```python
import functools
import math

import jax
import jax.numpy as jnp
from jax import lax
from jax.experimental import pallas as pl
from jax.experimental.pallas import tpu as pltpu
from jax.sharding import PartitionSpec as P

MESH = pl.DeviceIdType.MESH
BF = jnp.bfloat16
F32 = jnp.float32
LANES = 128
CORES = 2
GELU_A = math.sqrt(2.0 / math.pi)
GELU_B = 0.044715


def dot(a, b):
    return jnp.dot(a, b, preferred_element_type=F32)


def dot_nt(a, b):
    return lax.dot_general(a, b, (((1,), (1,)), ((), ())), preferred_element_type=F32)


def dot_tn(a, b):
    return lax.dot_general(a, b, (((0,), (0,)), ((), ())), preferred_element_type=F32)


def split(a):
    high = a.astype(BF)
    return high, (a - high.astype(F32)).astype(BF)


def gelu_parts(x):
    t = jnp.tanh(GELU_A * (x + GELU_B * x * x * x))
    value = 0.5 * x * (1.0 + t)
    slope = 0.5 * (1.0 + t) + 0.5 * x * (1.0 - t * t) * GELU_A * (1.0 + 3.0 * GELU_B * x * x)
    return value, slope


def ones_where(shape, test):
    rows = lax.broadcasted_iota(jnp.int32, shape, 0)
    cols = lax.broadcasted_iota(jnp.int32, shape, 1)
    return jnp.where(test(rows, cols), 1.0, 0.0).astype(BF)


def kernel(
    n_ex,
    n_chip,
    tasks,
    width,
    own_ref,
    labels_ref,
    w_in_hbm,
    w_out_hbm,
    gate_hbm,
    tower_hbm,
    bias_ref,
    out_ref,
    out_bias_ref,
    grad_in_ref,
    grad_out_ref,
    grad_gate_ref,
    first_buf,
    shuf,
    ev_a,
    ev_b,
    w_in_v,
    w_out_v,
    fused,
    tower_v,
    gate_v,
    gate_cat,
    part_own,
    part_send,
    part_recv,
    term_send,
    term_recv,
    small,
    prob_own,
    share_own,
    share,
    slope_v,
    hidden_t,
    ev_t,
    dt_chunk,
    dt_first,
    dt_a,
    dt_b,
    dg_chunk,
    dg_first,
    dg_a,
    dg_b,
    acc_in,
    acc_mid,
    acc_gate,
    load_sem,
    w_send,
    w_recv,
    first_send,
    first_recv,
    ev_send,
    ev_recv,
    evf_send,
    evf_recv,
    part_ssem,
    part_rsem,
    term_ssem,
    term_rsem,
    dt1_send,
    dt1_recv,
    dg1_send,
    dg1_recv,
    dt_send,
    dt_recv,
    dtf_send,
    dtf_recv,
    dg_send,
    dg_recv,
    dgf_send,
    dgf_recv,
):
    dp = lax.axis_index("dp")
    ex = lax.axis_index("expert")
    core = lax.rem(dp, CORES)
    chip = lax.div(dp, CORES)
    sibling = (dp + 1 - 2 * core, ex)
    feat = ev_a.shape[2]
    wide = tasks * width
    blk = ev_a.shape[1]
    hid = w_out_v.shape[0]
    gates = gate_cat.shape[1]
    experts = gates // tasks
    g_rows = ev_t.shape[2]
    per_group = g_rows // blk
    half = n_chip // per_group

    def ex_peer(k):
        return (dp, lax.rem(ex + k, n_ex))

    def chip_peer(k):
        return (lax.rem(chip + k, n_chip) * CORES + core, ex)

    def remote(src, dst, send, recv, to):
        return pltpu.make_async_remote_copy(
            src_ref=src, dst_ref=dst, send_sem=send, recv_sem=recv, device_id=to, device_id_type=MESH
        )

    barrier = pltpu.get_barrier_semaphore()

    @pl.loop(1, n_ex)
    def _(k):
        pl.semaphore_signal(barrier, inc=1, device_id=ex_peer(k), device_id_type=MESH)

    @pl.loop(1, n_chip)
    def _(k):
        pl.semaphore_signal(barrier, inc=1, device_id=chip_peer(k), device_id_type=MESH)

    pl.semaphore_signal(barrier, inc=1, device_id=sibling, device_id_type=MESH)

    loads = [
        pltpu.make_async_copy(src, dst, load_sem.at[i])
        for i, (src, dst) in enumerate(
            (
                (w_out_hbm.at[0], w_out_v),
                (tower_hbm, tower_v),
                (w_in_hbm.at[0], w_in_v.at[0]),
                (gate_hbm, gate_v),
            )
        )
    ]
    for load in loads:
        load.start()
    pl.semaphore_wait(barrier, n_ex + n_chip - 1)

    def spread(src_of, dst, send, recv):
        @pl.loop(1, n_ex)
        def _(k):
            to = ex_peer(k)
            remote(src_of(to[1]), dst.at[ex], send, recv, to).start()

    def spread_wait(dst, send, recv):
        every = dst.at[pl.ds(0, n_ex - 1)]
        copy = remote(every, every, send, recv, ex_peer(1))
        copy.wait_recv()
        copy.wait_send()

    def unshuffle(src, dst, count):
        rows = src.shape[1]
        shuf[pl.ds(0, n_ex * rows), :] = src[...].astype(F32).reshape(n_ex * rows, LANES)
        for j in range(count):
            for i in range(2):
                piece = shuf[pl.ds(j * 2 + i, n_ex, stride=rows), :]
                dst[i * n_ex : (i + 1) * n_ex, j * LANES : (j + 1) * LANES] = piece.astype(BF)

    spread(lambda _: own_ref, first_buf, first_send, first_recv)
    first_buf[ex] = own_ref[...]
    w_in_copy = remote(w_in_hbm.at[0], w_in_v.at[1], w_send.at[0], w_recv.at[0], sibling)
    w_in_copy.start()
    for t in range(tasks):
        for j in range(width // LANES):
            for i in range(2):
                at = (t * (width // LANES) + j) * 2 + i
                cols = slice(j * LANES, (j + 1) * LANES)
                small[0, at : at + 1, :] = bias_ref[t : t + 1, cols]
                small[1, at : at + 1, :] = out_ref[t : t + 1, cols]
    loads[0].wait()
    loads[1].wait()
    for t in range(tasks):
        cols = slice(t * width, (t + 1) * width)
        fused[0, :, cols] = dot(w_out_v[...], tower_v[t]).astype(BF)
    fused_copy = remote(fused.at[0], fused.at[1], w_send.at[1], w_recv.at[1], sibling)
    fused_copy.start()
    loads[3].wait()
    gate_cat[...] = jnp.concatenate([gate_v[t].astype(F32) for t in range(tasks)], axis=1).astype(BF)
    same_task = ones_where((gates, gates), lambda r, c: r // experts == c // experts)
    own_share = ones_where(
        (gates, wide), lambda r, c: (r // experts == c // width) & (r % experts == ex)
    )

    def gate_probs(rows):
        logits = dot(rows, gate_cat[...])
        lane = lax.broadcasted_iota(jnp.int32, logits.shape, 1) // experts
        top = jnp.zeros_like(logits)
        for t in range(tasks):
            mine = lane == t
            peak = jnp.max(jnp.where(mine, logits, -jnp.inf), axis=1, keepdims=True)
            top = jnp.where(mine, peak, top)
        grown = jnp.exp(logits - top)
        high, low = split(grown)
        return grown / (dot(high, same_task) + dot(low, same_task))

    def shares(probs):
        high, low = split(probs)
        return dot(high, own_share) + dot(low, own_share)

    spread_wait(first_buf, first_send, first_recv)
    unshuffle(first_buf, ev_a.at[chip], feat // LANES)

    def to_chips(buf, send, recv):
        @pl.loop(1, n_chip)
        def _(k):
            mine = buf.at[chip]
            remote(mine, buf.at[chip], send.at[k], recv.at[chip], chip_peer(k)).start()

    def arrived(buf, send, recv, slot):
        remote(buf.at[slot], buf.at[slot], send.at[0], recv.at[slot], sibling).wait_recv()

    def forward(buf, other, send, recv, slot):
        remote(buf.at[slot], other.at[slot], send.at[slot], recv.at[slot], sibling).start()

    def sends_done(buf, send, first, last):
        @pl.loop(first, last)
        def _(k):
            remote(buf.at[0], buf.at[0], send.at[k], send.at[k], sibling).wait_send()

    to_chips(ev_a, ev_send, ev_recv)
    forward(ev_a, ev_b, evf_send, evf_recv, chip)
    probs = gate_probs(ev_a[chip])
    prob_own[...] = probs
    share_own[...] = shares(probs)
    loads[2].wait()
    w_in_copy.wait_recv()
    fused_copy.wait_recv()

    def forward_block(slot):
        rows = ev_a[slot]
        part = None
        for h in range(2):
            pre = dot(rows, w_in_v[h])
            hidden = gelu_parts(pre)[0].astype(BF)
            term = dot(hidden, fused[h])
            part = term if part is None else part + term
        return part

    part_own[...] = forward_block(chip)

    @pl.loop(1, n_chip)
    def _(k):
        slot = lax.rem(chip + k, n_chip)
        arrived(ev_a, ev_send, ev_recv, slot)
        forward(ev_a, ev_b, evf_send, evf_recv, slot)
        part_send[slot] = forward_block(slot).astype(BF)
        remote(
            part_send.at[slot], part_recv.at[chip], part_ssem.at[k], part_rsem.at[chip], chip_peer(k)
        ).start()

    def prepare(group, buf, at):
        rows = buf[pl.ds(at * per_group, per_group)].reshape(g_rows, feat)
        pre = dot(rows, w_in_v[0])
        value, slope = gelu_parts(pre)
        slope_v[group] = slope
        hidden_t[group] = value.T.astype(BF)
        ev_t[group] = rows.astype(F32).T.astype(BF)
        share[group] = shares(gate_probs(rows))

    @pl.loop(0, half)
    def _(g):
        prepare(g, ev_a, g)

    @pl.loop(0, n_chip)
    def _(k):
        arrived(ev_b, evf_send, evf_recv, k)

    @pl.loop(0, half)
    def _(g):
        prepare(half + g, ev_b, g)

    total = part_own[...]
    for k in range(1, n_chip):
        slot = lax.rem(chip + k, n_chip)
        arrived(part_recv, part_ssem, part_rsem, slot)
        total = total + part_recv[slot].astype(F32)
    terms = total * share_own[...]
    crow = term_send.shape[1]
    for j in range(wide // LANES):
        for i in range(2):
            shuf[pl.ds(j * 2 + i, n_ex, stride=crow), :] = terms[
                i * n_ex : (i + 1) * n_ex, j * LANES : (j + 1) * LANES
            ]
    term_send[...] = shuf[pl.ds(0, n_ex * crow), :].reshape(n_ex, crow, LANES).astype(BF)
    spread(lambda to: term_send.at[to], term_recv, term_ssem, term_rsem)
    term_recv[ex] = term_send[ex]
    spread_wait(term_recv, term_ssem, term_rsem)

    def both_halves(value):
        row = lax.broadcasted_iota(jnp.int32, value.shape, 0)
        step = 2
        while step < 2 * (width // LANES):
            up = pltpu.roll(value, crow - step, 0)
            down = pltpu.roll(value, step, 0)
            value = value + jnp.where((row // step) % 2 == 0, up, down)
            step *= 2
        return value

    mixed = jnp.sum(term_recv[...].astype(F32), axis=0)
    act, act_slope = gelu_parts(mixed + small[0])
    weight = small[1]
    summed = jnp.broadcast_to(jnp.sum(act * weight, axis=1, keepdims=True), mixed.shape)
    row = lax.broadcasted_iota(jnp.int32, mixed.shape, 0)
    task_of = row // (2 * (width // LANES))
    logit = both_halves(summed)
    target = jnp.zeros_like(logit)
    for t in range(tasks):
        logit = logit + jnp.where(task_of == t, out_bias_ref[t], 0.0)
        for i in range(2):
            label = labels_ref[i, t].astype(F32)
            target = target + jnp.where((task_of == t) & (row % 2 == i), label, 0.0)
    dlogit = 1.0 / (1.0 + jnp.exp(-logit)) - target
    dt = (dlogit * weight * act_slope).astype(BF)
    dt_chunk[...] = dt
    spread(lambda _: dt_chunk, dt_first, dt1_send, dt1_recv)
    dt_first[ex] = dt

    prod = (term_recv[...].astype(F32) * dt.astype(F32)[None]).reshape(n_ex * crow, LANES)
    high, low = split(prod)
    all_ones = jnp.ones((LANES, gates), BF)
    sums = dot(high, all_ones) + dot(low, all_ones)
    at = lax.broadcasted_iota(jnp.int32, sums.shape, 0)
    lane = lax.broadcasted_iota(jnp.int32, sums.shape, 1)
    here = lane == (at % crow) // (2 * (width // LANES)) * experts + at // crow
    sums = jnp.where(here, sums, 0.0)
    pick = ones_where((16, n_ex * crow), lambda r, c: (r == c % 2))
    high, low = split(sums)
    moved = dot(pick, high) + dot(pick, low)
    high, low = split(moved)
    weighted = dot(high, same_task) + dot(low, same_task)
    own_rows = jnp.concatenate(
        [
            prob_own[pl.ds(ex, 1), :],
            prob_own[pl.ds(n_ex + ex, 1), :],
            jnp.zeros((14, gates), F32),
        ],
        axis=0,
    )
    dg = (moved - own_rows * weighted).astype(BF)
    dg_chunk[...] = dg
    spread(lambda _: dg_chunk, dg_first, dg1_send, dg1_recv)
    dg_first[ex] = dg

    spread_wait(dt_first, dt1_send, dt1_recv)
    unshuffle(dt_first, dt_a.at[chip], wide // LANES)
    to_chips(dt_a, dt_send, dt_recv)
    forward(dt_a, dt_b, dtf_send, dtf_recv, chip)
    spread_wait(dg_first, dg1_send, dg1_recv)
    rows16 = dg_first.shape[1]
    shuf2 = shuf.at[pl.ds(0, n_ex * rows16)]
    shuf2[:, 0:gates] = dg_first[...].astype(F32).reshape(n_ex * rows16, gates)
    for i in range(2):
        dg_a[chip, i * n_ex : (i + 1) * n_ex, :] = shuf2[pl.ds(i, n_ex, stride=rows16), :][
            :, 0:gates
        ].astype(BF)
    to_chips(dg_a, dg_send, dg_recv)
    forward(dg_a, dg_b, dgf_send, dgf_recv, chip)

    @pl.loop(1, n_chip)
    def _(k):
        slot = lax.rem(chip + k, n_chip)
        arrived(dt_a, dt_send, dt_recv, slot)
        forward(dt_a, dt_b, dtf_send, dtf_recv, slot)
        arrived(dg_a, dg_send, dg_recv, slot)
        forward(dg_a, dg_b, dgf_send, dgf_recv, slot)

    acc_in[...] = jnp.zeros_like(acc_in)
    acc_mid[...] = jnp.zeros_like(acc_mid)
    acc_gate[...] = jnp.zeros_like(acc_gate)

    def backward(group, ev_buf, dt_buf, dg_buf, at):
        span = pl.ds(at * per_group, per_group)
        dout = (dt_buf[span].reshape(g_rows, wide).astype(F32) * share[group]).astype(BF)
        dhidden = dot_nt(dout, fused[0])
        dpre = (dhidden * slope_v[group]).astype(BF)
        acc_in[...] += dot(ev_t[group], dpre)
        acc_mid[...] += dot(hidden_t[group], dout)
        rows = ev_buf[span].reshape(g_rows, feat)
        acc_gate[...] += dot(dg_buf[span].reshape(g_rows, gates).astype(F32).T.astype(BF), rows)

    @pl.loop(0, half)
    def _(g):
        backward(g, ev_a, dt_a, dg_a, g)

    @pl.loop(0, n_chip)
    def _(k):
        arrived(dt_b, dtf_send, dtf_recv, k)
        arrived(dg_b, dgf_send, dgf_recv, k)

    @pl.loop(0, half)
    def _(g):
        backward(half + g, ev_b, dt_b, dg_b, g)

    grad_in_ref[...] = acc_in[...].astype(BF)
    mid = acc_mid[...].astype(BF)
    result = None
    for t in range(tasks):
        term = dot_nt(mid[:, t * width : (t + 1) * width], tower_v[t])
        result = term if result is None else result + term
    grad_out_ref[...] = result.astype(BF)
    mine = ones_where((grad_gate_ref.shape[0], gates), lambda r, c: (c == r * experts + ex))
    high, low = split(acc_gate[...])
    grad_gate_ref[...] = dot(mine, high) + dot(mine, low)

    w_in_copy.wait_send()
    fused_copy.wait_send()
    for buf, send in (
        (ev_a, ev_send),
        (part_send, part_ssem),
        (dt_a, dt_send),
        (dg_a, dg_send),
    ):
        sends_done(buf, send, 1, n_chip)
    for buf, send in ((ev_a, evf_send), (dt_a, dtf_send), (dg_a, dgf_send)):
        sends_done(buf, send, 0, n_chip)


def per_device(
    n_dp,
    n_ex,
    events,
    labels,
    w_in,
    w_out,
    gate_weight,
    tower_in,
    tower_bias,
    tower_out,
    tower_out_bias,
):
    tasks, feat, width = tower_in.shape
    experts = gate_weight.shape[2]
    hid = w_out.shape[1]
    n_chip = n_dp // CORES
    own = events.shape[0]
    blk = own * n_ex
    plane = n_chip * blk
    g_rows = max(plane // 2, blk)
    groups = 2 * plane // g_rows
    wide = tasks * width
    gates = tasks * experts
    chunk = own * feat // LANES
    chunk_t = own * wide // LANES
    chunk_events = events.reshape(own, feat // LANES, LANES).transpose(1, 0, 2).reshape(chunk, LANES)
    vmem = pl.BlockSpec(memory_space=pltpu.VMEM)
    smem = pl.BlockSpec(memory_space=pltpu.SMEM)
    hbm = pl.BlockSpec(memory_space=pl.ANY)
    dma = pltpu.SemaphoreType.DMA
    scratch = [
        pltpu.VMEM((n_ex, chunk, LANES), BF),
        pltpu.VMEM((n_ex * max(chunk, chunk_t, 16), LANES), F32),
        pltpu.VMEM((n_chip, blk, feat), BF),
        pltpu.VMEM((n_chip, blk, feat), BF),
        pltpu.VMEM((2, feat, hid), BF),
        pltpu.VMEM((hid, feat), BF),
        pltpu.VMEM((2, hid, wide), BF),
        pltpu.VMEM((tasks, feat, width), BF),
        pltpu.VMEM((tasks, feat, experts), BF),
        pltpu.VMEM((feat, gates), BF),
        pltpu.VMEM((blk, wide), F32),
        pltpu.VMEM((n_chip, blk, wide), BF),
        pltpu.VMEM((n_chip, blk, wide), BF),
        pltpu.VMEM((n_ex, chunk_t, LANES), BF),
        pltpu.VMEM((n_ex, chunk_t, LANES), BF),
        pltpu.VMEM((2, chunk_t, LANES), F32),
        pltpu.VMEM((blk, gates), F32),
        pltpu.VMEM((blk, wide), F32),
        pltpu.VMEM((groups, g_rows, wide), F32),
        pltpu.VMEM((groups, g_rows, hid), F32),
        pltpu.VMEM((groups, hid, g_rows), BF),
        pltpu.VMEM((groups, feat, g_rows), BF),
        pltpu.VMEM((chunk_t, LANES), BF),
        pltpu.VMEM((n_ex, chunk_t, LANES), BF),
        pltpu.VMEM((n_chip, blk, wide), BF),
        pltpu.VMEM((n_chip, blk, wide), BF),
        pltpu.VMEM((16, gates), BF),
        pltpu.VMEM((n_ex, 16, gates), BF),
        pltpu.VMEM((n_chip, blk, gates), BF),
        pltpu.VMEM((n_chip, blk, gates), BF),
        pltpu.VMEM((feat, hid), F32),
        pltpu.VMEM((hid, wide), F32),
        pltpu.VMEM((gates, feat), F32),
        dma((4,)),
        dma((2,)),
        dma((2,)),
        dma,
        dma,
        dma((n_chip,)),
        dma((n_chip,)),
        dma((n_chip,)),
        dma((n_chip,)),
        dma((n_chip,)),
        dma((n_chip,)),
        dma,
        dma,
        dma,
        dma,
        dma,
        dma,
    ] + [dma((n_chip,))] * 8
    grad_in, grad_out, grad_gate = pl.pallas_call(
        functools.partial(kernel, n_ex, n_chip, tasks, width),
        out_shape=(
            jax.ShapeDtypeStruct((feat, hid), BF),
            jax.ShapeDtypeStruct((hid, feat), BF),
            jax.ShapeDtypeStruct((8, feat), F32),
        ),
        in_specs=[vmem, smem, hbm, hbm, hbm, hbm, vmem, vmem, smem],
        out_specs=(vmem, vmem, vmem),
        scratch_shapes=scratch,
        compiler_params=pltpu.CompilerParams(
            collective_id=0, has_side_effects=True, vmem_limit_bytes=48 * 1024 * 1024
        ),
    )(
        chunk_events,
        labels,
        w_in,
        w_out,
        gate_weight,
        tower_in,
        tower_bias,
        tower_out,
        tower_out_bias,
    )
    return grad_in[None], grad_out[None], grad_gate[:tasks, :, None]


def solution(mesh):
    placed = (
        P(("dp", "expert"), None),
        P(("dp", "expert"), None),
        P("expert", None, "dp"),
        P("expert", "dp", None),
        P(),
        P(),
        P(),
        P(),
        P(),
    )
    return jax.shard_map(
        functools.partial(per_device, mesh.shape["dp"], mesh.shape["expert"]),
        mesh=mesh,
        in_specs=placed,
        out_specs=(P("expert", None, "dp"), P("expert", "dp", None), P(None, None, "expert")),
        check_vma=False,
    )
```

time: 1700 us -> 102 us (0.06)
  waiting for transfers between devices: 1420 us -> 0 us
  blocking collectives: 231 us -> 0 us
  Pallas kernels: 0 us -> 90.2 us
  matrix products: 19.3 us -> 0 us
    all_gather x2 -> x0, waiting for transfers between devices: 1060 us -> none  [the longest x1 1060 us: per_device(): every = lax.all_gather(events, ('dp', 'expert'), axis=0, tiled=True)]
    unnamed x5 -> x0, waiting for transfers between devices: 296 us -> none
    psum x2 -> x0, blocking collectives: 161 us -> none  [the longest x1 97.6 us: per_device(): grad_gate = lax.psum(gate_part, 'dp')[:, :, None]]
    pallas_call x0 -> x1, Pallas kernels: none -> 90.2 us  [per_device(): pl.pallas_call(functools.partial(kernel, n_ex, n_chip, tasks, width), out...]
    all_gather x1 -> x0, blocking collectives: 70.3 us -> none  [per_device(): block_grads = lax.all_gather(dmixed, 'expert', axis=1, tiled=True)]
    reduce_scatter x1 -> x0, waiting for transfers between devices: 63.1 us -> none  [per_device(): lax.psum_scatter(jnp.dot(hidden, w_out[0], preferred_element_type=jnp.flo...]
    dot_general x9 -> x0, matrix products: 18.1 us -> none  [the longest x1 5.22 us: per_device(): lax.dot_general(every, dpre, (((0,), (0,)), ((), ())), preferred_element_...]
  transfers between devices with their start and end apart: 4 -> 0, of which waited for: 3 -> 0; matrix products, arithmetic and copies ran while one was open for 0% -> 0% of each run, Pallas kernels for 0% -> 0%
where the time goes in v1:
time: 102 us
  Pallas kernels  90.2 us (88%)
  local copies, waits for them, and re-layouts  10.7 us (10%)
    pallas_call x1, Pallas kernels, per_device(): pl.pallas_call(functools.partial(kernel, n_ex, n_chip, tasks, width), out...  90.2 us
    unnamed x20, local copies, waits for them, and re-layouts  10.7 us

profile of v1, /device:TPU:1, one launch (start us, length us, event | category | flops | bytes accessed | tf_op | source)
XLA Modules:
  0.0 101.6 jit_solution(12834091080643213911)
XLA Ops:
  0.6 1.4 %copy.13.gate_hbm = bf16[4,1024,32]{2,1,0:T(8,128)(2,1)S(1)} copy(bf16[4,1024,32]{1,2,0:T(8,128)(2,1)} %param.13) | data formatting | bytes 524288 | tf_op args[4]
  2.1 0.0 copy-start
  2.1 1.6 %copy-done = bf16[4,1024,256]{2,1,0:T(8,128)(2,1)S(1)} copy-done((bf16[4,1024,256]{2,1,0:T(8,128)(2,1)S(1)}, bf16[4,1024,256]{2,1,0:T(8,128)(2,1)}, u32[]{:S(2)}) %copy-start) | copy-done | bytes 2097176
  3.7 0.0 copy-start.1
  3.7 1.0 %copy-done.1 = bf16[1,1024,256]{2,1,0:T(8,128)(2,1)S(1)} copy-done((bf16[1,1024,256]{2,1,0:T(8,128)(2,1)S(1)}, bf16[1,1024,256]{2,1,0:T(8,128)(2,1)}, u32[]{:S(2)}) %copy-start.1) | copy-done | bytes 524312
  4.7 0.0 copy-start.2
  4.7 1.0 %copy-done.2 = bf16[1,256,1024]{2,1,0:T(8,128)(2,1)S(1)} copy-done((bf16[1,256,1024]{2,1,0:T(8,128)(2,1)S(1)}, bf16[1,256,1024]{2,1,0:T(8,128)(2,1)}, u32[]{:S(2)}) %copy-start.2) | copy-done | bytes 524312
  5.7 0.0 copy-start.3
  5.7 0.7 copy-done.3
  6.4 0.0 copy-start.4
  6.4 0.7 copy-done.4
  7.1 0.0 copy-start.5
  7.1 0.7 copy-done.5
  7.8 0.0 copy-start.6
  7.8 0.7 copy-done.6
  8.5 0.0 copy-start.7
  8.5 0.7 copy-done.7
  9.1 90.2 %shard_map.112 = (bf16[1024,256]{1,0:T(8,128)(2,1)S(1)}, bf16[256,1024]{1,0:T(8,128)(2,1)S(1)}, f32[8,1024]{1,0:T(8,128)S(1)}) custom-call(bf16[16,128]{1,0:T(8,128)(2,1)S(1)} %bitcast.11, s32[2,4]{1,0:T(2,128)S(1)} %copy-done.6, bf16[1,1024,256]{2,1,0:T(8,128)(2,1)S(1)} %copy-done.1, bf16[1,256,1024]{2,1,0:T(8,128)(2,1)S(1)} %copy-done.2, ...), custom_call_target="tpu_custom_call" | custom-call | tf_op jit(solution)/shard_map/pallas_call | solution.py:541
  99.4 0.6 copy.14
  100.0 0.8 copy.17
  100.8 0.8 copy.18
  (1 shorter events, 0.0 us)
Async XLA Ops:
  2.1 1.6 %copy-start = (bf16[4,1024,256]{2,1,0:T(8,128)(2,1)S(1)}, bf16[4,1024,256]{2,1,0:T(8,128)(2,1)}, u32[]{:S(2)}) copy-start(bf16[4,1024,256]{2,1,0:T(8,128)(2,1)} %tower_hbm.1) | copy-start | bytes 6291460
  3.7 1.0 %copy-start.1 = (bf16[1,1024,256]{2,1,0:T(8,128)(2,1)S(1)}, bf16[1,1024,256]{2,1,0:T(8,128)(2,1)}, u32[]{:S(2)}) copy-start(bf16[1,1024,256]{2,1,0:T(8,128)(2,1)} %w_in_hbm.1) | copy-start | bytes 1572868
  4.7 1.0 %copy-start.2 = (bf16[1,256,1024]{2,1,0:T(8,128)(2,1)S(1)}, bf16[1,256,1024]{2,1,0:T(8,128)(2,1)}, u32[]{:S(2)}) copy-start(bf16[1,256,1024]{2,1,0:T(8,128)(2,1)} %w_out_hbm.1) | copy-start | bytes 1572868
  5.7 0.7 copy-start.3
  6.4 0.7 copy-start.4
  7.1 0.7 copy-start.5
  7.8 0.7 copy-start.6
  8.5 0.7 copy-start.7

commit v2 on v1

--- a/solution.py
+++ b/solution.py
@@ -15,6 +15,7 @@
 CORES = 2
 GELU_A = math.sqrt(2.0 / math.pi)
 GELU_B = 0.044715
+VMEM_MIB = 34
 
 
 def dot(a, b):
@@ -52,15 +53,15 @@
     n_chip,
     tasks,
     width,
-    own_ref,
-    labels_ref,
+    own_hbm,
+    labels_hbm,
     w_in_hbm,
     w_out_hbm,
     gate_hbm,
     tower_hbm,
-    bias_ref,
-    out_ref,
-    out_bias_ref,
+    bias_hbm,
+    out_hbm,
+    out_bias_hbm,
     grad_in_ref,
     grad_out_ref,
     grad_gate_ref,
@@ -73,7 +74,10 @@
     fused,
     tower_v,
     gate_v,
-    gate_cat,
+    labels_v,
+    bias_v,
+    out_v,
+    out_bias_v,
     part_own,
     part_send,
     part_recv,
@@ -127,12 +131,17 @@
     ex = lax.axis_index("expert")
     core = lax.rem(dp, CORES)
     chip = lax.div(dp, CORES)
+    n_x = n_chip // 2
+    n_yh = min(4, n_ex)
+    n_z = n_ex // n_yh
+    x, y_lo = lax.rem(chip, n_x), lax.div(chip, n_x)
+    y = lax.div(ex, n_z) * 2 + y_lo
     sibling = (dp + 1 - 2 * core, ex)
     feat = ev_a.shape[2]
     wide = tasks * width
     blk = ev_a.shape[1]
     hid = w_out_v.shape[0]
-    gates = gate_cat.shape[1]
+    gates = gate_v.shape[0]
     experts = gates // tasks
     g_rows = ev_t.shape[2]
     per_group = g_rows // blk
@@ -144,6 +153,16 @@
     def chip_peer(k):
         return (lax.rem(chip + k, n_chip) * CORES + core, ex)
 
+    def x_peer(step):
+        return ((y_lo * n_x + lax.rem(x + step + n_x, n_x)) * CORES + core, ex)
+
+    def y_peer(step):
+        to = lax.rem(y + step + 2 * n_yh, 2 * n_yh)
+        return (
+            (lax.rem(to, 2) * n_x + x) * CORES + core,
+            lax.div(to, 2) * n_z + lax.rem(ex, n_z),
+        )
+
     def remote(src, dst, send, recv, to):
         return pltpu.make_async_remote_copy(
             src_ref=src, dst_ref=dst, send_sem=send, recv_sem=recv, device_id=to, device_id_type=MESH
@@ -160,6 +179,7 @@
         pl.semaphore_signal(barrier, inc=1, device_id=chip_peer(k), device_id_type=MESH)
 
     pl.semaphore_signal(barrier, inc=1, device_id=sibling, device_id_type=MESH)
+    pl.semaphore_signal(barrier, inc=1, device_id=y_peer(2 * y_lo - 1), device_id_type=MESH)
 
     loads = [
         pltpu.make_async_copy(src, dst, load_sem.at[i])
@@ -169,12 +189,17 @@
                 (tower_hbm, tower_v),
                 (w_in_hbm.at[0], w_in_v.at[0]),
                 (gate_hbm, gate_v),
+                (labels_hbm, labels_v),
+                (bias_hbm, bias_v),
+                (out_hbm, out_v),
+                (out_bias_hbm, out_bias_v),
+                (own_hbm, first_buf.at[ex]),
             )
         )
     ]
     for load in loads:
         load.start()
-    pl.semaphore_wait(barrier, n_ex + n_chip - 1)
+    pl.semaphore_wait(barrier, n_ex + n_chip)
 
     def spread(src_of, dst, send, recv):
         @pl.loop(1, n_ex)
@@ -196,17 +221,21 @@
                 piece = shuf[pl.ds(j * 2 + i, n_ex, stride=rows), :]
                 dst[i * n_ex : (i + 1) * n_ex, j * LANES : (j + 1) * LANES] = piece.astype(BF)
 
-    spread(lambda _: own_ref, first_buf, first_send, first_recv)
-    first_buf[ex] = own_ref[...]
+    spread(lambda _: own_hbm, first_buf, first_send, first_recv)
     w_in_copy = remote(w_in_hbm.at[0], w_in_v.at[1], w_send.at[0], w_recv.at[0], sibling)
     w_in_copy.start()
+    for load in loads[4:9]:
+        load.wait()
     for t in range(tasks):
         for j in range(width // LANES):
+            at = (t * (width // LANES) + j) * 2
+            cols = slice(j * LANES, (j + 1) * LANES)
             for i in range(2):
-                at = (t * (width // LANES) + j) * 2 + i
-                cols = slice(j * LANES, (j + 1) * LANES)
-                small[0, at : at + 1, :] = bias_ref[t : t + 1, cols]
-                small[1, at : at + 1, :] = out_ref[t : t + 1, cols]
+                small[0, at + i : at + i + 1, :] = bias_v[t : t + 1, cols]
+                small[1, at + i : at + i + 1, :] = out_v[t : t + 1, cols]
+            label = labels_v[:, t : t + 1].astype(F32)
+            small[2, at : at + 2, :] = jnp.broadcast_to(label, (2, LANES))
+            small[3, at : at + 2, :] = jnp.broadcast_to(out_bias_v[:, t : t + 1], (2, LANES))
     loads[0].wait()
     loads[1].wait()
     for t in range(tasks):
@@ -215,14 +244,13 @@
     fused_copy = remote(fused.at[0], fused.at[1], w_send.at[1], w_recv.at[1], sibling)
     fused_copy.start()
     loads[3].wait()
-    gate_cat[...] = jnp.concatenate([gate_v[t].astype(F32) for t in range(tasks)], axis=1).astype(BF)
     same_task = ones_where((gates, gates), lambda r, c: r // experts == c // experts)
     own_share = ones_where(
         (gates, wide), lambda r, c: (r // experts == c // width) & (r % experts == ex)
     )
 
     def gate_probs(rows):
-        logits = dot(rows, gate_cat[...])
+        logits = dot_nt(rows, gate_v[...])
         lane = lax.broadcasted_iota(jnp.int32, logits.shape, 1) // experts
         top = jnp.zeros_like(logits)
         for t in range(tasks):
@@ -257,8 +285,102 @@
         def _(k):
             remote(buf.at[0], buf.at[0], send.at[k], send.at[k], sibling).wait_send()
 
-    to_chips(ev_a, ev_send, ev_recv)
-    forward(ev_a, ev_b, evf_send, evf_recv, chip)
+    rows_half = blk // 2
+    left = y_lo * n_x + lax.rem(x + n_x - 1, n_x)
+    right = y_lo * n_x + lax.rem(x + 1, n_x)
+    across = y_lo * n_x + lax.rem(x + 2, n_x)
+    other_row = (1 - 2 * y_lo) * n_x
+
+    class Gather:
+        def __init__(self, buf, twin, send, recv, twin_send, twin_recv):
+            self.buf, self.twin, self.send, self.recv = buf, twin, send, recv
+            self.twin_send, self.twin_recv = twin_send, twin_recv
+
+        def half(self, slot, h, buf=None):
+            buf = self.buf if buf is None else buf
+            return buf.at[slot, pl.ds(h * rows_half, rows_half)]
+
+        def push(self, slot, h, to, sem):
+            ref = self.half(slot, h)
+            remote(ref, ref, self.send.at[sem], self.recv.at[slot, h], to).start()
+
+        def got(self, slot, h):
+            ref = self.half(slot, h)
+            remote(ref, ref, self.send.at[0], self.recv.at[slot, h], sibling).wait_recv()
+
+        def pass_on(self, slot, h):
+            remote(
+                self.half(slot, h),
+                self.half(slot, h, self.twin),
+                self.twin_send.at[slot, h],
+                self.twin_recv.at[slot, h],
+                sibling,
+            ).start()
+
+        def begin(self):
+            self.push(chip, 0, x_peer(1), 0)
+            self.push(chip, 1, x_peer(-1), 1)
+            self.push(chip, 0, y_peer(1), 2)
+            self.push(chip, 1, y_peer(-1), 3)
+            self.push(chip, 1, x_peer(1), 4)
+            self.push(chip, 0, x_peer(-1), 5)
+            self.pass_on(chip, 0)
+            self.pass_on(chip, 1)
+
+        def sides(self):
+            self.got(left, 0)
+            self.push(left, 0, x_peer(1), 6)
+            self.push(left, 0, y_peer(1), 7)
+            self.got(right, 1)
+            self.push(right, 1, x_peer(-1), 8)
+            self.push(right, 1, y_peer(-1), 9)
+            self.got(left, 1)
+            self.push(left, 1, y_peer(-1), 10)
+            self.got(right, 0)
+            self.push(right, 0, y_peer(1), 11)
+            for slot in (left, right):
+                self.pass_on(slot, 0)
+                self.pass_on(slot, 1)
+
+        def opposite(self):
+            self.got(across, 0)
+            self.push(across, 0, y_peer(1), 12)
+            self.got(across, 1)
+            self.push(across, 1, y_peer(-1), 13)
+            self.pass_on(across, 0)
+            self.pass_on(across, 1)
+
+        def other(self, slot):
+            slot = slot + other_row
+            for h in range(2):
+                self.got(slot, h)
+                self.pass_on(slot, h)
+            return slot
+
+        def twin_row(self, first):
+            @pl.loop(0, n_x)
+            def _(k):
+                for h in range(2):
+                    ref = self.half(first + k, h, self.twin)
+                    remote(
+                        ref, ref, self.send.at[0], self.twin_recv.at[first + k, h], sibling
+                    ).wait_recv()
+
+        def sent(self):
+            ref = self.half(0, 0)
+
+            @pl.loop(0, 14)
+            def _(k):
+                remote(ref, ref, self.send.at[k], self.recv.at[0, 0], sibling).wait_send()
+
+            @pl.loop(0, n_chip)
+            def _(k):
+                for h in range(2):
+                    sem = self.twin_send.at[k, h]
+                    remote(ref, ref, sem, self.recv.at[0, 0], sibling).wait_send()
+
+    events = Gather(ev_a, ev_b, ev_send, ev_recv, evf_send, evf_recv)
+    events.begin()
     probs = gate_probs(ev_a[chip])
     prob_own[...] = probs
     share_own[...] = shares(probs)
@@ -276,17 +398,23 @@
             part = term if part is None else part + term
         return part
 
+    def send_part(slot, sem):
+        part_send[slot] = forward_block(slot).astype(BF)
+        to = (slot * CORES + core, ex)
+        remote(
+            part_send.at[slot], part_recv.at[chip], part_ssem.at[sem], part_rsem.at[chip], to
+        ).start()
+
     part_own[...] = forward_block(chip)
-
-    @pl.loop(1, n_chip)
-    def _(k):
-        slot = lax.rem(chip + k, n_chip)
-        arrived(ev_a, ev_send, ev_recv, slot)
-        forward(ev_a, ev_b, evf_send, evf_recv, slot)
-        part_send[slot] = forward_block(slot).astype(BF)
-        remote(
-            part_send.at[slot], part_recv.at[chip], part_ssem.at[k], part_rsem.at[chip], chip_peer(k)
-        ).start()
+    events.sides()
+    send_part(left, 1)
+    send_part(right, 2)
+    events.opposite()
+    send_part(across, 3)
+    send_part(events.other(chip), 4)
+    send_part(events.other(left), 5)
+    send_part(events.other(right), 6)
+    send_part(events.other(across), 7)
 
     def prepare(group, buf, at):
         rows = buf[pl.ds(at * per_group, per_group)].reshape(g_rows, feat)
@@ -301,9 +429,8 @@
     def _(g):
         prepare(g, ev_a, g)
 
-    @pl.loop(0, n_chip)
-    def _(k):
-        arrived(ev_b, evf_send, evf_recv, k)
+    events.twin_row(0)
+    events.twin_row(n_x)
 
     @pl.loop(0, half)
     def _(g):
@@ -340,16 +467,8 @@
     act, act_slope = gelu_parts(mixed + small[0])
     weight = small[1]
     summed = jnp.broadcast_to(jnp.sum(act * weight, axis=1, keepdims=True), mixed.shape)
-    row = lax.broadcasted_iota(jnp.int32, mixed.shape, 0)
-    task_of = row // (2 * (width // LANES))
-    logit = both_halves(summed)
-    target = jnp.zeros_like(logit)
-    for t in range(tasks):
-        logit = logit + jnp.where(task_of == t, out_bias_ref[t], 0.0)
-        for i in range(2):
-            label = labels_ref[i, t].astype(F32)
-            target = target + jnp.where((task_of == t) & (row % 2 == i), label, 0.0)
-    dlogit = 1.0 / (1.0 + jnp.exp(-logit)) - target
+    logit = both_halves(summed) + small[3]
+    dlogit = 1.0 / (1.0 + jnp.exp(-logit)) - small[2]
     dt = (dlogit * weight * act_slope).astype(BF)
     dt_chunk[...] = dt
     spread(lambda _: dt_chunk, dt_first, dt1_send, dt1_recv)
@@ -383,8 +502,8 @@
 
     spread_wait(dt_first, dt1_send, dt1_recv)
     unshuffle(dt_first, dt_a.at[chip], wide // LANES)
-    to_chips(dt_a, dt_send, dt_recv)
-    forward(dt_a, dt_b, dtf_send, dtf_recv, chip)
+    towers = Gather(dt_a, dt_b, dt_send, dt_recv, dtf_send, dtf_recv)
+    towers.begin()
     spread_wait(dg_first, dg1_send, dg1_recv)
     rows16 = dg_first.shape[1]
     shuf2 = shuf.at[pl.ds(0, n_ex * rows16)]
@@ -396,40 +515,50 @@
     to_chips(dg_a, dg_send, dg_recv)
     forward(dg_a, dg_b, dgf_send, dgf_recv, chip)
 
-    @pl.loop(1, n_chip)
-    def _(k):
-        slot = lax.rem(chip + k, n_chip)
-        arrived(dt_a, dt_send, dt_recv, slot)
-        forward(dt_a, dt_b, dtf_send, dtf_recv, slot)
-        arrived(dg_a, dg_send, dg_recv, slot)
-        forward(dg_a, dg_b, dgf_send, dgf_recv, slot)
-
     acc_in[...] = jnp.zeros_like(acc_in)
     acc_mid[...] = jnp.zeros_like(acc_mid)
     acc_gate[...] = jnp.zeros_like(acc_gate)
 
-    def backward(group, ev_buf, dt_buf, dg_buf, at):
+    def backward(group, dt_buf, at):
         span = pl.ds(at * per_group, per_group)
         dout = (dt_buf[span].reshape(g_rows, wide).astype(F32) * share[group]).astype(BF)
         dhidden = dot_nt(dout, fused[0])
         dpre = (dhidden * slope_v[group]).astype(BF)
         acc_in[...] += dot(ev_t[group], dpre)
         acc_mid[...] += dot(hidden_t[group], dout)
+
+    def gate_rows(ev_buf, dg_buf, at):
+        span = pl.ds(at * per_group, per_group)
         rows = ev_buf[span].reshape(g_rows, feat)
         acc_gate[...] += dot(dg_buf[span].reshape(g_rows, gates).astype(F32).T.astype(BF), rows)
 
-    @pl.loop(0, half)
-    def _(g):
-        backward(g, ev_a, dt_a, dg_a, g)
+    towers.sides()
+    towers.opposite()
+    backward(y_lo, dt_a, y_lo)
+
+    @pl.loop(1, n_chip)
+    def _(k):
+        slot = lax.rem(chip + k, n_chip)
+        arrived(dg_a, dg_send, dg_recv, slot)
+        forward(dg_a, dg_b, dgf_send, dgf_recv, slot)
+
+    towers.other(chip)
+    towers.other(left)
+    towers.other(right)
+    towers.twin_row(y_lo * n_x)
+    backward(half + y_lo, dt_b, y_lo)
+    towers.other(across)
+    backward(1 - y_lo, dt_a, 1 - y_lo)
 
     @pl.loop(0, n_chip)
     def _(k):
-        arrived(dt_b, dtf_send, dtf_recv, k)
         arrived(dg_b, dgf_send, dgf_recv, k)
 
-    @pl.loop(0, half)
-    def _(g):
-        backward(half + g, ev_b, dt_b, dg_b, g)
+    for g in range(half):
+        gate_rows(ev_a, dg_a, g)
+        gate_rows(ev_b, dg_b, g)
+    towers.twin_row((1 - y_lo) * n_x)
+    backward(half + 1 - y_lo, dt_b, 1 - y_lo)
 
     grad_in_ref[...] = acc_in[...].astype(BF)
     mid = acc_mid[...].astype(BF)
@@ -438,21 +567,31 @@
         term = dot_nt(mid[:, t * width : (t + 1) * width], tower_v[t])
         result = term if result is None else result + term
     grad_out_ref[...] = result.astype(BF)
-    mine = ones_where((grad_gate_ref.shape[0], gates), lambda r, c: (c == r * experts + ex))
+    mine = ones_where((16, gates), lambda r, c: (c == r * experts + ex))
     high, low = split(acc_gate[...])
-    grad_gate_ref[...] = dot(mine, high) + dot(mine, low)
+    gate_sums = dot(mine, high) + dot(mine, low)
+    for t in range(tasks):
+        grad_gate_ref[t] = gate_sums[t : t + 1]
 
     w_in_copy.wait_send()
     fused_copy.wait_send()
-    for buf, send in (
-        (ev_a, ev_send),
-        (part_send, part_ssem),
-        (dt_a, dt_send),
-        (dg_a, dg_send),
-    ):
+    events.sent()
+    towers.sent()
+    for buf, send in ((part_send, part_ssem), (dg_a, dg_send)):
         sends_done(buf, send, 1, n_chip)
-    for buf, send in ((ev_a, evf_send), (dt_a, dtf_send), (dg_a, dgf_send)):
-        sends_done(buf, send, 0, n_chip)
+    sends_done(dg_a, dgf_send, 0, n_chip)
+
+
+def place(*refs):
+    count = (len(refs) - 1) // 2
+    sem = refs[-1]
+    copies = [
+        pltpu.make_async_copy(refs[i], refs[count + i], sem.at[i]) for i in range(count)
+    ]
+    for copy in copies:
+        copy.start()
+    for copy in copies:
+        copy.wait()
 
 
 def per_device(
@@ -483,8 +622,7 @@
     chunk_t = own * wide // LANES
     chunk_events = events.reshape(own, feat // LANES, LANES).transpose(1, 0, 2).reshape(chunk, LANES)
     vmem = pl.BlockSpec(memory_space=pltpu.VMEM)
-    smem = pl.BlockSpec(memory_space=pltpu.SMEM)
-    hbm = pl.BlockSpec(memory_space=pl.ANY)
+    hbm = pl.BlockSpec(memory_space=pltpu.HBM)
     dma = pltpu.SemaphoreType.DMA
     scratch = [
         pltpu.VMEM((n_ex, chunk, LANES), BF),
@@ -495,14 +633,17 @@
         pltpu.VMEM((hid, feat), BF),
         pltpu.VMEM((2, hid, wide), BF),
         pltpu.VMEM((tasks, feat, width), BF),
-        pltpu.VMEM((tasks, feat, experts), BF),
-        pltpu.VMEM((feat, gates), BF),
+        pltpu.VMEM((gates, feat), BF),
+        pltpu.VMEM((own, tasks), jnp.int32),
+        pltpu.VMEM((tasks, width), F32),
+        pltpu.VMEM((tasks, width), F32),
+        pltpu.VMEM((1, tasks), F32),
         pltpu.VMEM((blk, wide), F32),
         pltpu.VMEM((n_chip, blk, wide), BF),
         pltpu.VMEM((n_chip, blk, wide), BF),
         pltpu.VMEM((n_ex, chunk_t, LANES), BF),
         pltpu.VMEM((n_ex, chunk_t, LANES), BF),
-        pltpu.VMEM((2, chunk_t, LANES), F32),
+        pltpu.VMEM((4, chunk_t, LANES), F32),
         pltpu.VMEM((blk, gates), F32),
         pltpu.VMEM((blk, wide), F32),
         pltpu.VMEM((groups, g_rows, wide), F32),
@@ -520,15 +661,15 @@
         pltpu.VMEM((feat, hid), F32),
         pltpu.VMEM((hid, wide), F32),
         pltpu.VMEM((gates, feat), F32),
-        dma((4,)),
+        dma((9,)),
         dma((2,)),
         dma((2,)),
         dma,
         dma,
-        dma((n_chip,)),
-        dma((n_chip,)),
-        dma((n_chip,)),
-        dma((n_chip,)),
+        dma((14,)),
+        dma((n_chip, 2)),
+        dma((n_chip, 2)),
+        dma((n_chip, 2)),
         dma((n_chip,)),
         dma((n_chip,)),
         dma,
@@ -537,32 +678,52 @@
         dma,
         dma,
         dma,
-    ] + [dma((n_chip,))] * 8
-    grad_in, grad_out, grad_gate = pl.pallas_call(
+        dma((14,)),
+        dma((n_chip, 2)),
+        dma((n_chip, 2)),
+        dma((n_chip, 2)),
+        dma((n_chip,)),
+        dma((n_chip,)),
+        dma((n_chip,)),
+        dma((n_chip,)),
+    ]
+    results = pl.pallas_call(
         functools.partial(kernel, n_ex, n_chip, tasks, width),
         out_shape=(
             jax.ShapeDtypeStruct((feat, hid), BF),
             jax.ShapeDtypeStruct((hid, feat), BF),
-            jax.ShapeDtypeStruct((8, feat), F32),
+            jax.ShapeDtypeStruct((tasks, 1, feat), F32),
         ),
-        in_specs=[vmem, smem, hbm, hbm, hbm, hbm, vmem, vmem, smem],
+        in_specs=[hbm] * 9,
         out_specs=(vmem, vmem, vmem),
         scratch_shapes=scratch,
         compiler_params=pltpu.CompilerParams(
-            collective_id=0, has_side_effects=True, vmem_limit_bytes=48 * 1024 * 1024
+            collective_id=0, has_side_effects=True, vmem_limit_bytes=VMEM_MIB * 1024 * 1024
         ),
     )(
-        chunk_events,
-        labels,
-        w_in,
-        w_out,
-        gate_weight,
-        tower_in,
-        tower_bias,
-        tower_out,
-        tower_out_bias,
+        *(
+            pltpu.with_memory_space_constraint(operand, pltpu.HBM)
+            for operand in (
+                chunk_events,
+                labels,
+                w_in,
+                w_out,
+                gate_weight.transpose(0, 2, 1).reshape(gates, feat),
+                tower_in,
+                tower_bias,
+                tower_out,
+                tower_out_bias.reshape(1, tasks),
+            )
+        )
     )
-    return grad_in[None], grad_out[None], grad_gate[:tasks, :, None]
+    grad_in, grad_out, grad_gate = pl.pallas_call(
+        place,
+        out_shape=[jax.ShapeDtypeStruct(r.shape, r.dtype) for r in results],
+        in_specs=[pl.BlockSpec(memory_space=pl.ANY)] * len(results),
+        out_specs=[hbm] * len(results),
+        scratch_shapes=[dma((len(results),))],
+    )(*results)
+    return grad_in[None], grad_out[None], grad_gate.transpose(0, 2, 1)
 
 
 def solution(mesh):

time: 102 us -> 117 us (1.15)
  Pallas kernels: 90.2 us -> 114 us
  local copies, waits for them, and re-layouts: 10.7 us -> 2.18 us
    pallas_call x0 -> x1, Pallas kernels: none -> 33.4 us  [per_device(): pl.pallas_call(place, out_shape=[jax.ShapeDtypeStruct(r.shape, r.dtype) f...]
    pallas_call x1, Pallas kernels: 90.2 us -> 80.7 us  [per_device(): pl.pallas_call(functools.partial(kernel, n_ex, n_chip, tasks, width), out...]
    unnamed x20 -> x6, local copies, waits for them, and re-layouts: 10.7 us -> 2.18 us
where the time goes in v2:
time: 117 us
  Pallas kernels  114 us (97%)
  local copies, waits for them, and re-layouts  2.18 us (2%)
    pallas_call x1, Pallas kernels, per_device(): pl.pallas_call(functools.partial(kernel, n_ex, n_chip, tasks, width), out...  80.7 us
    pallas_call x1, Pallas kernels, per_device(): pl.pallas_call(place, out_shape=[jax.ShapeDtypeStruct(r.shape, r.dtype) f...  33.4 us

profile of v2, /device:TPU:1, one launch (start us, length us, event | category | flops | bytes accessed | tf_op | source)
XLA Modules:
  0.0 117.0 jit_solution(4999714168048673853)
XLA Ops:
  0.6 80.7 %shard_map.112 = (bf16[1024,256]{1,0:T(8,128)(2,1)S(1)}, bf16[256,1024]{1,0:T(8,128)(2,1)S(1)}, f32[4,1,1024]{2,1,0:T(1,128)S(1)}) custom-call(bf16[16,128]{1,0:T(8,128)(2,1)} %bitcast.13, s32[2,4]{1,0:T(2,128)} %labels_hbm.1, bf16[1,1024,256]{2,1,0:T(8,128)(2,1)} %w_in_hbm.1, bf16[1,256,1024]{2,1,0:T(8,128)(2,1)} %w_out_hbm.1, bf16[128,1024]{1,0:T(8,128)(2,1)} %bitcast.12, ...), custom_call_target="tpu_custom_call" | custom-call | tf_op jit(solution)/shard_map/pallas_call | solution.py:690
  81.4 0.0 copy-start
  81.4 0.8 copy-done
  82.2 0.0 copy-start.1
  82.2 0.8 copy-done.1
  83.0 0.0 copy-start.2
  83.0 0.6 copy-done.2
  83.6 33.4 %shard_map.113 = (bf16[1024,256]{1,0:T(8,128)(2,1)}, bf16[256,1024]{1,0:T(8,128)(2,1)}, f32[4,1,1024]{2,1,0:T(1,128)}) custom-call(bf16[1024,256]{1,0:T(8,128)(2,1)} %copy-done, bf16[256,1024]{1,0:T(8,128)(2,1)} %copy-done.1, f32[4,1,1024]{2,1,0:T(1,128)} %copy-done.2), custom_call_target="tpu_custom_call" | custom-call | tf_op jit(solution)/shard_map/pallas_call | solution.py:719
Async XLA Ops:
  81.4 0.8 copy-start
  82.2 0.8 copy-start.1
  83.0 0.6 copy-start.2

commit v3 on v2

--- a/solution.py
+++ b/solution.py
@@ -16,6 +16,8 @@
 GELU_A = math.sqrt(2.0 / math.pi)
 GELU_B = 0.044715
 VMEM_MIB = 34
+EV_PARTS = 2
+DT_PARTS = 2
 
 
 def dot(a, b):
@@ -135,7 +137,8 @@
     n_yh = min(4, n_ex)
     n_z = n_ex // n_yh
     x, y_lo = lax.rem(chip, n_x), lax.div(chip, n_x)
-    y = lax.div(ex, n_z) * 2 + y_lo
+    y_hi, z = lax.div(ex, n_z), lax.rem(ex, n_z)
+    y = y_hi * 2 + y_lo
     sibling = (dp + 1 - 2 * core, ex)
     feat = ev_a.shape[2]
     wide = tasks * width
@@ -201,11 +204,13 @@
         load.start()
     pl.semaphore_wait(barrier, n_ex + n_chip)
 
+    steps = [(a, b) for a in range(n_yh) for b in range(n_z) if a or b]
+    steps.sort(key=lambda s: -(2 * min(s[0], n_yh - s[0]) + min(s[1], n_z - s[1])))
+
     def spread(src_of, dst, send, recv):
-        @pl.loop(1, n_ex)
-        def _(k):
-            to = ex_peer(k)
-            remote(src_of(to[1]), dst.at[ex], send, recv, to).start()
+        for a, b in steps:
+            to_ex = lax.rem(y_hi + a, n_yh) * n_z + lax.rem(z + b, n_z)
+            remote(src_of(to_ex), dst.at[ex], send, recv, (dp, to_ex)).start()
 
     def spread_wait(dst, send, recv):
         every = dst.at[pl.ds(0, n_ex - 1)]
@@ -285,101 +290,98 @@
         def _(k):
             remote(buf.at[0], buf.at[0], send.at[k], send.at[k], sibling).wait_send()
 
-    rows_half = blk // 2
     left = y_lo * n_x + lax.rem(x + n_x - 1, n_x)
     right = y_lo * n_x + lax.rem(x + 1, n_x)
     across = y_lo * n_x + lax.rem(x + 2, n_x)
     other_row = (1 - 2 * y_lo) * n_x
 
     class Gather:
-        def __init__(self, buf, twin, send, recv, twin_send, twin_recv):
+        def __init__(self, parts, buf, twin, send, recv, twin_send, twin_recv):
             self.buf, self.twin, self.send, self.recv = buf, twin, send, recv
             self.twin_send, self.twin_recv = twin_send, twin_recv
-
-        def half(self, slot, h, buf=None):
-            buf = self.buf if buf is None else buf
-            return buf.at[slot, pl.ds(h * rows_half, rows_half)]
-
-        def push(self, slot, h, to, sem):
-            ref = self.half(slot, h)
-            remote(ref, ref, self.send.at[sem], self.recv.at[slot, h], to).start()
-
-        def got(self, slot, h):
-            ref = self.half(slot, h)
-            remote(ref, ref, self.send.at[0], self.recv.at[slot, h], sibling).wait_recv()
-
-        def pass_on(self, slot, h):
+            self.rows = blk // parts
+            self.up = list(range(parts // 2))
+            self.down = list(range(parts // 2, parts))
+            self.count = 0
+
+        def part(self, slot, p):
+            return self.buf.at[slot, pl.ds(p * self.rows, self.rows)]
+
+        def push(self, slot, p, to):
+            ref = self.part(slot, p)
+            remote(ref, ref, self.send.at[self.count], self.recv.at[slot, p], to).start()
+            self.count += 1
+
+        def got(self, slot, p):
+            ref = self.part(slot, p)
+            remote(ref, ref, self.send.at[0], self.recv.at[slot, p], sibling).wait_recv()
+
+        def pass_on(self, slot):
             remote(
-                self.half(slot, h),
-                self.half(slot, h, self.twin),
-                self.twin_send.at[slot, h],
-                self.twin_recv.at[slot, h],
+                self.buf.at[slot],
+                self.twin.at[slot],
+                self.twin_send.at[slot],
+                self.twin_recv.at[slot],
                 sibling,
             ).start()
 
         def begin(self):
-            self.push(chip, 0, x_peer(1), 0)
-            self.push(chip, 1, x_peer(-1), 1)
-            self.push(chip, 0, y_peer(1), 2)
-            self.push(chip, 1, y_peer(-1), 3)
-            self.push(chip, 1, x_peer(1), 4)
-            self.push(chip, 0, x_peer(-1), 5)
-            self.pass_on(chip, 0)
-            self.pass_on(chip, 1)
+            for u, d in zip(self.up, self.down):
+                self.push(chip, u, x_peer(1))
+                self.push(chip, d, x_peer(-1))
+                self.push(chip, u, y_peer(1))
+                self.push(chip, d, y_peer(-1))
+            for u, d in zip(self.up, self.down):
+                self.push(chip, d, x_peer(1))
+                self.push(chip, u, x_peer(-1))
+            self.pass_on(chip)
 
         def sides(self):
-            self.got(left, 0)
-            self.push(left, 0, x_peer(1), 6)
-            self.push(left, 0, y_peer(1), 7)
-            self.got(right, 1)
-            self.push(right, 1, x_peer(-1), 8)
-            self.push(right, 1, y_peer(-1), 9)
-            self.got(left, 1)
-            self.push(left, 1, y_peer(-1), 10)
-            self.got(right, 0)
-            self.push(right, 0, y_peer(1), 11)
-            for slot in (left, right):
-                self.pass_on(slot, 0)
-                self.pass_on(slot, 1)
+            for u, d in zip(self.up, self.down):
+                self.got(left, u)
+                self.push(left, u, x_peer(1))
+                self.push(left, u, y_peer(1))
+                self.got(right, d)
+                self.push(right, d, x_peer(-1))
+                self.push(right, d, y_peer(-1))
+            for u, d in zip(self.up, self.down):
+                self.got(left, d)
+                self.push(left, d, y_peer(-1))
+                self.got(right, u)
+                self.push(right, u, y_peer(1))
+            self.pass_on(left)
+            self.pass_on(right)
 
         def opposite(self):
-            self.got(across, 0)
-            self.push(across, 0, y_peer(1), 12)
-            self.got(across, 1)
-            self.push(across, 1, y_peer(-1), 13)
-            self.pass_on(across, 0)
-            self.pass_on(across, 1)
+            for u, d in zip(self.up, self.down):
+                self.got(across, u)
+                self.push(across, u, y_peer(1))
+                self.got(across, d)
+                self.push(across, d, y_peer(-1))
+            self.pass_on(across)
 
         def other(self, slot):
             slot = slot + other_row
-            for h in range(2):
-                self.got(slot, h)
-                self.pass_on(slot, h)
+            for p in self.up + self.down:
+                self.got(slot, p)
+            self.pass_on(slot)
             return slot
 
         def twin_row(self, first):
             @pl.loop(0, n_x)
             def _(k):
-                for h in range(2):
-                    ref = self.half(first + k, h, self.twin)
-                    remote(
-                        ref, ref, self.send.at[0], self.twin_recv.at[first + k, h], sibling
-                    ).wait_recv()
+                arrived(self.twin, self.send, self.twin_recv, first + k)
 
         def sent(self):
-            ref = self.half(0, 0)
-
-            @pl.loop(0, 14)
+            ref = self.part(0, 0)
+
+            @pl.loop(0, self.count)
             def _(k):
                 remote(ref, ref, self.send.at[k], self.recv.at[0, 0], sibling).wait_send()
 
-            @pl.loop(0, n_chip)
-            def _(k):
-                for h in range(2):
-                    sem = self.twin_send.at[k, h]
-                    remote(ref, ref, sem, self.recv.at[0, 0], sibling).wait_send()
-
-    events = Gather(ev_a, ev_b, ev_send, ev_recv, evf_send, evf_recv)
+            sends_done(self.buf, self.twin_send, 0, n_chip)
+
+    events = Gather(EV_PARTS, ev_a, ev_b, ev_send, ev_recv, evf_send, evf_recv)
     events.begin()
     probs = gate_probs(ev_a[chip])
     prob_own[...] = probs
@@ -406,12 +408,12 @@
         ).start()
 
     part_own[...] = forward_block(chip)
+    send_part(events.other(chip), 4)
     events.sides()
     send_part(left, 1)
     send_part(right, 2)
     events.opposite()
     send_part(across, 3)
-    send_part(events.other(chip), 4)
     send_part(events.other(left), 5)
     send_part(events.other(right), 6)
     send_part(events.other(across), 7)
@@ -502,7 +504,7 @@
 
     spread_wait(dt_first, dt1_send, dt1_recv)
     unshuffle(dt_first, dt_a.at[chip], wide // LANES)
-    towers = Gather(dt_a, dt_b, dt_send, dt_recv, dtf_send, dtf_recv)
+    towers = Gather(DT_PARTS, dt_a, dt_b, dt_send, dt_recv, dtf_send, dtf_recv)
     towers.begin()
     spread_wait(dg_first, dg1_send, dg1_recv)
     rows16 = dg_first.shape[1]
@@ -533,8 +535,6 @@
         acc_gate[...] += dot(dg_buf[span].reshape(g_rows, gates).astype(F32).T.astype(BF), rows)
 
     towers.sides()
-    towers.opposite()
-    backward(y_lo, dt_a, y_lo)
 
     @pl.loop(1, n_chip)
     def _(k):
@@ -542,21 +542,29 @@
         arrived(dg_a, dg_send, dg_recv, slot)
         forward(dg_a, dg_b, dgf_send, dgf_recv, slot)
 
+    for g in range(half):
+        gate_rows(ev_a, dg_a, g)
+    towers.opposite()
+    backward(y_lo, dt_a, y_lo)
     towers.other(chip)
     towers.other(left)
     towers.other(right)
     towers.twin_row(y_lo * n_x)
     backward(half + y_lo, dt_b, y_lo)
-    towers.other(across)
-    backward(1 - y_lo, dt_a, 1 - y_lo)
 
     @pl.loop(0, n_chip)
     def _(k):
         arrived(dg_b, dgf_send, dgf_recv, k)
 
     for g in range(half):
-        gate_rows(ev_a, dg_a, g)
         gate_rows(ev_b, dg_b, g)
+    towers.other(across)
+    backward(1 - y_lo, dt_a, 1 - y_lo)
+    mine = ones_where((16, gates), lambda r, c: (c == r * experts + ex))
+    high, low = split(acc_gate[...])
+    gate_sums = dot(mine, high) + dot(mine, low)
+    for t in range(tasks):
+        grad_gate_ref[t] = gate_sums[t : t + 1]
     towers.twin_row((1 - y_lo) * n_x)
     backward(half + 1 - y_lo, dt_b, 1 - y_lo)
 
@@ -567,12 +575,6 @@
         term = dot_nt(mid[:, t * width : (t + 1) * width], tower_v[t])
         result = term if result is None else result + term
     grad_out_ref[...] = result.astype(BF)
-    mine = ones_where((16, gates), lambda r, c: (c == r * experts + ex))
-    high, low = split(acc_gate[...])
-    gate_sums = dot(mine, high) + dot(mine, low)
-    for t in range(tasks):
-        grad_gate_ref[t] = gate_sums[t : t + 1]
-
     w_in_copy.wait_send()
     fused_copy.wait_send()
     events.sent()
@@ -580,18 +582,6 @@
     for buf, send in ((part_send, part_ssem), (dg_a, dg_send)):
         sends_done(buf, send, 1, n_chip)
     sends_done(dg_a, dgf_send, 0, n_chip)
-
-
-def place(*refs):
-    count = (len(refs) - 1) // 2
-    sem = refs[-1]
-    copies = [
-        pltpu.make_async_copy(refs[i], refs[count + i], sem.at[i]) for i in range(count)
-    ]
-    for copy in copies:
-        copy.start()
-    for copy in copies:
-        copy.wait()
 
 
 def per_device(
@@ -666,10 +656,10 @@
         dma((2,)),
         dma,
         dma,
-        dma((14,)),
-        dma((n_chip, 2)),
-        dma((n_chip, 2)),
-        dma((n_chip, 2)),
+        dma((7 * EV_PARTS,)),
+        dma((n_chip, EV_PARTS)),
+        dma((n_chip,)),
+        dma((n_chip,)),
         dma((n_chip,)),
         dma((n_chip,)),
         dma,
@@ -678,16 +668,16 @@
         dma,
         dma,
         dma,
-        dma((14,)),
-        dma((n_chip, 2)),
-        dma((n_chip, 2)),
-        dma((n_chip, 2)),
+        dma((7 * DT_PARTS,)),
+        dma((n_chip, DT_PARTS)),
+        dma((n_chip,)),
+        dma((n_chip,)),
         dma((n_chip,)),
         dma((n_chip,)),
         dma((n_chip,)),
         dma((n_chip,)),
     ]
-    results = pl.pallas_call(
+    grad_in, grad_out, grad_gate = pl.pallas_call(
         functools.partial(kernel, n_ex, n_chip, tasks, width),
         out_shape=(
             jax.ShapeDtypeStruct((feat, hid), BF),
@@ -716,13 +706,6 @@
             )
         )
     )
-    grad_in, grad_out, grad_gate = pl.pallas_call(
-        place,
-        out_shape=[jax.ShapeDtypeStruct(r.shape, r.dtype) for r in results],
-        in_specs=[pl.BlockSpec(memory_space=pl.ANY)] * len(results),
-        out_specs=[hbm] * len(results),
-        scratch_shapes=[dma((len(results),))],
-    )(*results)
     return grad_in[None], grad_out[None], grad_gate.transpose(0, 2, 1)
 
 

time: 117 us -> 82.2 us (0.70)
  Pallas kernels: 114 us -> 79.2 us
    pallas_call x1 -> x0, Pallas kernels: 33.4 us -> none  [per_device(): pl.pallas_call(place, out_shape=[jax.ShapeDtypeStruct(r.shape, r.dtype) f...]
    pallas_call x1, Pallas kernels: 80.7 us -> 79.2 us  [per_device(): pl.pallas_call(functools.partial(kernel, n_ex, n_chip, tasks, width), out...]
where the time goes in v3:
time: 82.2 us; the launch traced here: 82.1 us
  Pallas kernels  79.2 us (96%)
  local copies, waits for them, and re-layouts  2.19 us (3%)
    pallas_call x1, Pallas kernels, per_device(): pl.pallas_call(functools.partial(kernel, n_ex, n_chip, tasks, width), out...  79.2 us
    unnamed x3, local copies, waits for them, and re-layouts  2.19 us

profile of v3, /device:TPU:1, one launch (start us, length us, event | category | flops | bytes accessed | tf_op | source)
XLA Modules:
  0.0 82.1 jit_solution(10012683819496923100)
XLA Ops:
  0.6 79.2 %shard_map.112 = (bf16[1024,256]{1,0:T(8,128)(2,1)S(1)}, bf16[256,1024]{1,0:T(8,128)(2,1)S(1)}, f32[4,1,1024]{2,1,0:T(1,128)S(1)}) custom-call(bf16[16,128]{1,0:T(8,128)(2,1)} %bitcast.16, s32[2,4]{1,0:T(2,128)} %labels_hbm.1, bf16[1,1024,256]{2,1,0:T(8,128)(2,1)} %w_in_hbm.1, bf16[1,256,1024]{2,1,0:T(8,128)(2,1)} %w_out_hbm.1, bf16[128,1024]{1,0:T(8,128)(2,1)} %bitcast.15, ...), custom_call_target="tpu_custom_call" | custom-call | tf_op jit(solution)/shard_map/pallas_call | solution.py:680
  79.9 0.8 copy.16
  80.7 0.8 copy.17
  81.5 0.6 copy.18

commit v4 on v3

--- a/solution.py
+++ b/solution.py
@@ -171,6 +171,8 @@
             src_ref=src, dst_ref=dst, send_sem=send, recv_sem=recv, device_id=to, device_id_type=MESH
         )
 
+    own_load = pltpu.make_async_copy(own_hbm, first_buf.at[ex], load_sem.at[8])
+    own_load.start()
     barrier = pltpu.get_barrier_semaphore()
 
     @pl.loop(1, n_ex)
@@ -196,7 +198,6 @@
                 (bias_hbm, bias_v),
                 (out_hbm, out_v),
                 (out_bias_hbm, out_bias_v),
-                (own_hbm, first_buf.at[ex]),
             )
         )
     ]
@@ -226,10 +227,11 @@
                 piece = shuf[pl.ds(j * 2 + i, n_ex, stride=rows), :]
                 dst[i * n_ex : (i + 1) * n_ex, j * LANES : (j + 1) * LANES] = piece.astype(BF)
 
-    spread(lambda _: own_hbm, first_buf, first_send, first_recv)
+    own_load.wait()
+    spread(lambda _: first_buf.at[ex], first_buf, first_send, first_recv)
     w_in_copy = remote(w_in_hbm.at[0], w_in_v.at[1], w_send.at[0], w_recv.at[0], sibling)
     w_in_copy.start()
-    for load in loads[4:9]:
+    for load in loads[4:8]:
         load.wait()
     for t in range(tasks):
         for j in range(width // LANES):
@@ -502,6 +504,11 @@
     spread(lambda _: dg_chunk, dg_first, dg1_send, dg1_recv)
     dg_first[ex] = dg
 
+    w_in_copy.wait_send()
+    fused_copy.wait_send()
+    events.sent()
+    sends_done(part_send, part_ssem, 1, n_chip)
+
     spread_wait(dt_first, dt1_send, dt1_recv)
     unshuffle(dt_first, dt_a.at[chip], wide // LANES)
     towers = Gather(DT_PARTS, dt_a, dt_b, dt_send, dt_recv, dtf_send, dtf_recv)
@@ -565,6 +572,9 @@
     gate_sums = dot(mine, high) + dot(mine, low)
     for t in range(tasks):
         grad_gate_ref[t] = gate_sums[t : t + 1]
+    sends_done(dg_a, dg_send, 1, n_chip)
+    sends_done(dg_a, dgf_send, 0, n_chip)
+    towers.sent()
     towers.twin_row((1 - y_lo) * n_x)
     backward(half + 1 - y_lo, dt_b, 1 - y_lo)
 
@@ -575,13 +585,6 @@
         term = dot_nt(mid[:, t * width : (t + 1) * width], tower_v[t])
         result = term if result is None else result + term
     grad_out_ref[...] = result.astype(BF)
-    w_in_copy.wait_send()
-    fused_copy.wait_send()
-    events.sent()
-    towers.sent()
-    for buf, send in ((part_send, part_ssem), (dg_a, dg_send)):
-        sends_done(buf, send, 1, n_chip)
-    sends_done(dg_a, dgf_send, 0, n_chip)
 
 
 def per_device(

time: 82.2 us -> 80 us (0.973)
  Pallas kernels: 79.2 us -> 77 us
    pallas_call x1, Pallas kernels: 79.2 us -> 77 us  [per_device(): pl.pallas_call(functools.partial(kernel, n_ex, n_chip, tasks, width), out...]
where the time goes in v4:
time: 80 us; the launch traced here: 79.9 us
  Pallas kernels  77 us (96%)
  local copies, waits for them, and re-layouts  2.19 us (3%)
    pallas_call x1, Pallas kernels, per_device(): pl.pallas_call(functools.partial(kernel, n_ex, n_chip, tasks, width), out...  77 us
    unnamed x3, local copies, waits for them, and re-layouts  2.19 us

profile of v4, /device:TPU:1, one launch (start us, length us, event | category | flops | bytes accessed | tf_op | source)
XLA Modules:
  0.0 79.9 jit_solution(14179211609889397914)
XLA Ops:
  0.6 77.0 %shard_map.112 = (bf16[1024,256]{1,0:T(8,128)(2,1)S(1)}, bf16[256,1024]{1,0:T(8,128)(2,1)S(1)}, f32[4,1,1024]{2,1,0:T(1,128)S(1)}) custom-call(bf16[16,128]{1,0:T(8,128)(2,1)} %bitcast.16, s32[2,4]{1,0:T(2,128)} %labels_hbm.1, bf16[1,1024,256]{2,1,0:T(8,128)(2,1)} %w_in_hbm.1, bf16[1,256,1024]{2,1,0:T(8,128)(2,1)} %w_out_hbm.1, bf16[128,1024]{1,0:T(8,128)(2,1)} %bitcast.15, ...), custom_call_target="tpu_custom_call" | custom-call | tf_op jit(solution)/shard_map/pallas_call | solution.py:683
  77.7 0.8 copy.16
  78.5 0.8 copy.17
  79.2 0.6 copy.18
